TPU v7x, 256 devices: a whole 4x4x8 slice. The times are simulated.
256 devices in a mesh: space: 32 (over z, x), state: 8 (over y, core).
Axes of the slice: x: 4, y: 4, z: 8, core: 2. Of those that a mesh axis runs over, the one named last changes fastest.
Arguments:
- states: float32 [64, 524288], P('state', 'space')
- bounds: float32 [3], replicated, as said below
- element_matrix: float32 [250, 125], replicated
- elem_nodes: int32 [125, 8192], P(None, 'space'), may hold values from 0 to 20479, as said below
- face_nodes: int32 [131072], P('space'), may hold values from 0 to 16383, as said below
- kinetic: float32 [8192], P('space'), may hold values from 0.5 to 4
- potential: float32 [8192], P('space'), may hold values from -1 to 0.5
- elem_count: int32 [32], P('space'), may hold values from 64 to 256, as said below
Outputs:
- filtered: float32 [64, 524288], P('state', 'space')
- margin: float32 [64, 64], P('state')
Inputs may be any that keep to these rules, and one draw needn't show every extreme that they name: `elem_nodes`: within each partition's 256 columns, rows 0 to 99 of a column are local node indices below 16384, and rows 100 to 124 are 16384 plus a face position below 4096. The entries of one column are distinct. `face_nodes`: within each partition's 4096 entries, distinct local node indices. `elem_count`: some partition has all 256 slots live in every draw. `bounds`: a0 < lo < hi.
All inputs are finite; a program needn't handle non-finite values.
Results may differ from a plain program's by a relative error of at most 0.0018.
Values may be sent and summed in bfloat16 or wider, within the bound.
A program may use at most 128 MiB of HBM per device.

v0:
```python
import jax
import jax.numpy as jnp
from jax import lax
from jax.sharding import PartitionSpec as P

DEG = 4


def shifted(value, axis, steps):
    count = lax.axis_size(axis)
    initial, last = (max(0, -steps), min(count, count - steps))
    return lax.ppermute(value, axis, [(source, source + steps) for source in range(initial, last)])


def hamiltonian(current, elem_nodes, face_nodes, kin_live, pot_live, element_matrix):
    width = current.shape[0]
    owned_count = current.shape[1]
    face_count = face_nodes.shape[0]
    corner_count = element_matrix.shape[1]
    face_vals = current[:, face_nodes]
    ghosts = shifted(face_vals.astype(jnp.bfloat16), "space", -1).astype(face_vals.dtype)
    extended = jnp.concatenate([current, ghosts], axis=1)
    gathered = extended[:, elem_nodes]
    product = jnp.einsum("kb,sbe->ske", element_matrix, gathered, precision=lax.Precision.HIGHEST)
    contrib = kin_live * product[:, :corner_count] + pot_live * product[:, corner_count:]
    summed = (
        jnp.zeros((width, owned_count + face_count), jnp.float32).at[:, elem_nodes].add(contrib)
    )
    returned = shifted(summed[:, owned_count:].astype(jnp.bfloat16), "space", 1).astype(jnp.float32)
    return summed[:, :owned_count].at[:, face_nodes].add(returned)


def body(states, bounds, element_matrix, elem_nodes, face_nodes, kinetic, potential, elem_count):
    slot_ids = jnp.arange(kinetic.shape[0], dtype=jnp.int32)
    alive = (slot_ids < elem_count[0]).astype(jnp.float32)
    kin_live = 0.5 * kinetic * alive
    pot_live = potential * alive

    def apply_operator(block):
        return hamiltonian(block, elem_nodes, face_nodes, kin_live, pot_live, element_matrix)

    lowest, lower, upper = (bounds[0], bounds[1], bounds[2])
    half_width = (upper - lower) / 2.0
    center = (upper + lower) / 2.0
    sigma_now = half_width / (lowest - center)
    gamma_ratio = 2.0 / sigma_now
    previous = states
    current = (apply_operator(states) - center * states) * (sigma_now / half_width)
    for repeat in range(DEG - 1):
        sigma_next = 1.0 / (gamma_ratio - sigma_now)
        following = (apply_operator(current) - center * current) * (
            2.0 * sigma_next / half_width
        ) - sigma_now * sigma_next * previous
        previous = current
        current = following
        sigma_now = sigma_next
    rounded = current.astype(jnp.bfloat16)
    node_total = current.shape[1] * lax.axis_size("space")
    partial_rows = lax.dot_general(
        rounded,
        lax.all_gather(rounded, "state", axis=0, tiled=True),
        (((1,), (1,)), ((), ())),
        preferred_element_type=jnp.float32,
    )
    margin = lax.psum(partial_rows, "space") / node_total
    return (current, margin)


def solution(mesh):
    in_specs = (
        P("state", "space"),
        P(),
        P(),
        P(None, "space"),
        P("space"),
        P("space"),
        P("space"),
        P("space"),
    )
    out_specs = (P("state", "space"), P("state", None))
    return jax.shard_map(body, mesh=mesh, in_specs=in_specs, out_specs=out_specs, check_vma=False)
```

profile of v0, /device:TPU:8, one launch (start us, length us, event | category | flops | bytes accessed | tf_op | source)
XLA Modules:
  0.0 1493.6 jit_solution(14101269677599258316)
XLA Ops:
  8.0 4.0 copy.113
  12.0 13.8 gather_fusion
  29.7 2.5 collective-permute-done
  33.3 5.4 copy.115
  38.7 63.1 %gather_fusion.1 = f32[32000,8]{1,0:T(8,128)} fusion(f32[8,20480]{0,1:T(8,128)} %copy.115, s32[32768]{0:T(1024)S(1)} %pad_clamp_fusion), kind=kCustom, calls=%fused_computation.1 | custom fusion | bytes 2176000 | tf_op jit(solution)/shard_map/gather | solution.py:23
  101.8 9.6 copy.116
  111.4 1.8 convolution_bitcast_fusion.3
  114.2 8.7 copy.118
  122.9 176.8 %scatter_custom_fusion = f32[8,20480]{0,1:T(8,128)} fusion(s32[32000]{0:T(1024)S(1)} %reshape.126, f32[32000,8]{1,0:T(8,128)} %copy.118, f32[]{:T(128)} %constant.7.clone.1), kind=kCustom, calls=%fused_computation.22 | custom fusion | flops 256000 | bytes 655872 | tf_op jit(solution)/shard_map/scatter-add | solution.py:27
  299.7 1.7 slice.99
  301.7 3.7 collective-permute-start.1
  309.4 5.7 slice.98
  315.2 2.0 copy.120
  317.2 27.0 %scatter_fusion = f32[8,16384]{0,1:T(8,128)} fusion(f32[8,16384]{0,1:T(8,128)} %slice.98, s32[4096]{0:T(1024)S(1)} %get-tuple-element.12, f32[4096,8]{1,0:T(8,128)} %copy.120), kind=kCustom, calls=%fused_computation.9 | custom fusion | flops 32768 | bytes 409600 | tf_op jit(solution)/shard_map/scatter-add | solution.py:30
  344.2 5.5 copy.121
  349.8 3.6 copy.122
  353.4 13.8 gather_fusion.2
  368.8 4.9 collective-permute-done.2
  373.7 5.4 copy.124
  379.1 63.1 %gather_fusion.3 = f32[32000,8]{1,0:T(8,128)} fusion(f32[8,20480]{0,1:T(8,128)} %copy.124, s32[32768]{0:T(1024)S(1)} %pad_clamp_fusion), kind=kCustom, calls=%fused_computation.3 | custom fusion | bytes 2176000 | tf_op jit(solution)/shard_map/gather | solution.py:23
  442.2 9.6 copy.125
  451.8 1.8 convolution_bitcast_fusion.2
  455.4 9.0 copy.127
  464.5 176.8 %scatter_custom_fusion.2 = f32[8,20480]{0,1:T(8,128)} fusion(s32[32000]{0:T(1024)S(1)} %reshape.126, f32[32000,8]{1,0:T(8,128)} %copy.127, f32[]{:T(128)} %constant.7.clone.1), kind=kCustom, calls=%fused_computation.20 | custom fusion | flops 256000 | bytes 655872 | tf_op jit(solution)/shard_map/scatter-add | solution.py:27
  641.3 1.7 slice.103
  643.3 4.7 collective-permute-start.3
  648.1 5.7 slice.102
  653.9 2.0 copy.129
  655.9 37.7 %scatter_fusion.1 = f32[8,16384]{0,1:T(8,128)} fusion(f32[8,16384]{0,1:T(8,128)} %slice.102, s32[4096]{0:T(1024)S(1)} %get-tuple-element.12, f32[4096,8]{1,0:T(8,128)} %copy.129), kind=kCustom, calls=%fused_computation.11 | custom fusion | flops 32768 | bytes 409600 | tf_op jit(solution)/shard_map/scatter-add | solution.py:30
  693.6 5.6 copy.130
  699.3 3.6 copy.131
  702.9 13.8 gather_fusion.4
  718.2 4.9 collective-permute-done.4
  723.2 5.4 copy.133
  728.6 63.1 %gather_fusion.5 = f32[32000,8]{1,0:T(8,128)} fusion(f32[8,20480]{0,1:T(8,128)} %copy.133, s32[32768]{0:T(1024)S(1)} %pad_clamp_fusion), kind=kCustom, calls=%fused_computation.5 | custom fusion | bytes 2176000 | tf_op jit(solution)/shard_map/gather | solution.py:23
  791.7 9.6 copy.134
  801.3 1.8 convolution_bitcast_fusion.1
  804.0 8.7 copy.136
  812.8 176.8 %scatter_custom_fusion.4 = f32[8,20480]{0,1:T(8,128)} fusion(s32[32000]{0:T(1024)S(1)} %reshape.126, f32[32000,8]{1,0:T(8,128)} %copy.136, f32[]{:T(128)} %constant.7.clone.1), kind=kCustom, calls=%fused_computation.18 | custom fusion | flops 256000 | bytes 655872 | tf_op jit(solution)/shard_map/scatter-add | solution.py:27
  989.6 1.7 slice.107
  991.6 4.1 collective-permute-start.5
  995.8 5.7 slice.106
  1001.5 2.0 copy.138
  1003.5 27.0 %scatter_fusion.2 = f32[8,16384]{0,1:T(8,128)} fusion(f32[8,16384]{0,1:T(8,128)} %slice.106, s32[4096]{0:T(1024)S(1)} %get-tuple-element.12, f32[4096,8]{1,0:T(8,128)} %copy.138), kind=kCustom, calls=%fused_computation.13 | custom fusion | flops 32768 | bytes 409600 | tf_op jit(solution)/shard_map/scatter-add | solution.py:30
  1030.5 5.5 copy.139
  1036.2 3.6 copy.140
  1039.8 13.8 gather_fusion.6
  1053.8 1.5 collective-permute-start.6
  1055.3 4.6 collective-permute-done.6
  1060.1 5.4 copy.142
  1065.4 63.1 %gather_fusion.7 = f32[32000,8]{1,0:T(8,128)} fusion(f32[8,20480]{0,1:T(8,128)} %copy.142, s32[32768]{0:T(1024)S(1)} %pad_clamp_fusion), kind=kCustom, calls=%fused_computation.7 | custom fusion | bytes 2176000 | tf_op jit(solution)/shard_map/gather | solution.py:23
  1128.5 9.6 copy.143
  1138.2 1.8 convolution_bitcast_fusion
  1141.8 9.0 copy.145
  1150.8 176.8 %scatter_custom_fusion.6 = f32[8,20480]{0,1:T(8,128)} fusion(s32[32000]{0:T(1024)S(1)} %reshape.126, f32[32000,8]{1,0:T(8,128)} %copy.145, f32[]{:T(128)} %constant.7.clone.1), kind=kCustom, calls=%fused_computation.16 | custom fusion | flops 256000 | bytes 655872 | tf_op jit(solution)/shard_map/scatter-add | solution.py:27
  1327.6 1.7 slice.111
  1329.6 4.0 collective-permute-start.7
  1333.8 5.7 slice.110
  1339.5 2.0 copy.147
  1341.5 27.0 %scatter_fusion.3 = f32[8,16384]{0,1:T(8,128)} fusion(f32[8,16384]{0,1:T(8,128)} %slice.110, s32[4096]{0:T(1024)S(1)} %get-tuple-element.12, f32[4096,8]{1,0:T(8,128)} %copy.147), kind=kCustom, calls=%fused_computation.15 | custom fusion | flops 32768 | bytes 409600 | tf_op jit(solution)/shard_map/scatter-add | solution.py:30
  1368.5 5.5 copy.148
  1375.1 33.3 %all-gather.2.cloned.1.call-done = bf16[64,16384]{1,0:T(8,128)(2,1)} async-done(((bf16[8,16384]{1,0:T(8,128)(2,1)}), bf16[64,16384]{1,0:T(8,128)(2,1)}) %all-gather.2.cloned.1.call-update) | async-done | bytes 2097168 | tf_op jit(solution)/shard_map/all_gather | solution.py:61
  1408.3 2.3 fusion.27
  1410.7 75.1 %psum.7 = f32[8,64]{1,0:T(8,128)S(1)} all-reduce(f32[8,64]{1,0:T(8,128)S(1)} %fusion.27), channel_id=1, replica_groups=mesh['space'=32,'state'=8] {'space'}, use_global_device_ids=true, to_apply=%region_8.0 | all-reduce | flops 512 | bytes 4096 | tf_op jit(solution)/shard_map/psum | solution.py:65
  (54 shorter events, 18.1 us)
Async XLA Ops:
  7.2 104.3 %copy-start = (f32[250,125]{1,0:T(8,128)S(1)}, f32[250,125]{1,0:T(8,128)}, u32[]{:S(2)}) copy-start(f32[250,125]{1,0:T(8,128)} %param.10) | copy-start | bytes 375004
  7.2 1401.2 %all-gather.2.cloned.1.call-start = ((), (), s32[]{:S(2)}) async-start(), calls=%async_computation | async-start | bytes 2359296 | tf_op jit(solution)/shard_map/all_gather | solution.py:61
  26.1 6.2 collective-permute-start
  122.9 182.5 %copy-start.2 = (f32[3]{0:T(128)S(1)}, f32[3]{0:T(128)}, u32[]{:S(2)}) copy-start(f32[3]{0:T(128)} %param.9) | copy-start | bytes 40
  301.7 13.4 collective-permute-start.1
  315.1 34.6 %copy-start.1 = (f32[8,16384]{1,0:T(8,128)S(1)}, f32[8,16384]{1,0:T(8,128)}, u32[]{:S(2)}) copy-start(f32[8,16384]{1,0:T(8,128)} %param.8) | copy-start | bytes 1572868
  367.5 6.2 collective-permute-start.2
  643.3 10.6 collective-permute-start.3
  716.9 6.2 collective-permute-start.4
  991.6 9.9 collective-permute-start.5
  1053.8 6.2 collective-permute-start.6
  1329.6 9.8 collective-permute-start.7
Sparse Core Ops, SparseCore 0:
  1375.2 33.0 all-gather.1
where the time goes:
time: 1500 us; the launch traced here: 1490 us
  other arithmetic  833 us (56%)
  local copies, waits for them, and re-layouts  484 us (32%)
  blocking collectives  75.1 us (5%)
  waiting for transfers between devices  50.2 us (3%)
  starting transfers between devices  21.9 us (1%)
  between operations  19.2 us (1%)
    scatter-add x4, other arithmetic, hamiltonian(): jnp.zeros((width, owned_count + face_count), jnp.float32).at[:, elem_nodes]  707 us
    gather x8, local copies, waits for them, and re-layouts, hamiltonian(): gathered = extended[:, elem_nodes]  291 us
    scatter-add x4, other arithmetic, hamiltonian(): return summed[:, :owned_count].at[:, face_nodes].add(returned)  119 us
    psum x1, blocking collectives, body(): margin = lax.psum(partial_rows, 'space') / node_total  75.1 us
    gather x4, local copies, waits for them, and re-layouts, hamiltonian(): face_vals = current[:, face_nodes]  55 us
    add x8, local copies, waits for them, and re-layouts, hamiltonian(): kin_live * product[:, :corner_count] + pot_live * product[:, corner_count:]  39.3 us
    all_gather x1, waiting for transfers between devices, body(): lax.all_gather(rounded, 'state', axis=0, tiled=True)  33.3 us
  transfers between devices with their start and end apart: 9, of which 5 were waited for; matrix products, arithmetic and copies ran while one was open for 2% of the time, Pallas kernels for 0%

commit v1 on v0

--- a/solution.py
+++ b/solution.py
@@ -62,7 +62,7 @@
         (((1,), (1,)), ((), ())),
         preferred_element_type=jnp.float32,
     )
-    margin = lax.psum(partial_rows, "space") / node_total
+    margin = jnp.sum(lax.all_gather(partial_rows, "space"), axis=0) / node_total
     return (current, margin)
 
 

time: 1500 us -> 1470 us (0.980)
  blocking collectives: 75.1 us -> 44.1 us
    psum x1 -> x0, blocking collectives: 75.1 us -> none  [body(): margin = lax.psum(partial_rows, 'space') / node_total]
    all_gather x0 -> x1, blocking collectives: none -> 44.1 us  [body(): margin = jnp.sum(lax.all_gather(partial_rows, 'space'), axis=0) / node_total]
where the time goes in v1:
time: 1470 us; the launch traced here: 1460 us
  other arithmetic  833 us (57%)
  local copies, waits for them, and re-layouts  484 us (33%)
  waiting for transfers between devices  50.2 us (3%)
  blocking collectives  44.1 us (3%)
  starting transfers between devices  21.9 us (1%)
  between operations  19.2 us (1%)
    scatter-add x4, other arithmetic, hamiltonian(): jnp.zeros((width, owned_count + face_count), jnp.float32).at[:, elem_nodes]  707 us
    gather x8, local copies, waits for them, and re-layouts, hamiltonian(): gathered = extended[:, elem_nodes]  291 us
    scatter-add x4, other arithmetic, hamiltonian(): return summed[:, :owned_count].at[:, face_nodes].add(returned)  119 us
    gather x4, local copies, waits for them, and re-layouts, hamiltonian(): face_vals = current[:, face_nodes]  55 us
    all_gather x1, blocking collectives, body(): margin = jnp.sum(lax.all_gather(partial_rows, 'space'), axis=0) / node_total  44.1 us
    add x8, local copies, waits for them, and re-layouts, hamiltonian(): kin_live * product[:, :corner_count] + pot_live * product[:, corner_count:]  39.3 us
    all_gather x1, waiting for transfers between devices, body(): lax.all_gather(rounded, 'state', axis=0, tiled=True)  33.3 us
  transfers between devices with their start and end apart: 9, of which 5 were waited for; matrix products, arithmetic and copies ran while one was open for 2% of the time, Pallas kernels for 0%

profile of v1, /device:TPU:8, one launch (start us, length us, event | category | flops | bytes accessed | tf_op | source)
XLA Modules:
  0.0 1462.6 jit_solution(17761905250028139426)
XLA Ops:
  8.0 4.0 copy.113
  12.0 13.8 gather_fusion
  29.7 2.5 collective-permute-done
  33.3 5.4 copy.115
  38.7 63.1 %gather_fusion.1 = f32[32000,8]{1,0:T(8,128)} fusion(f32[8,20480]{0,1:T(8,128)} %copy.115, s32[32768]{0:T(1024)S(1)} %pad_clamp_fusion), kind=kCustom, calls=%fused_computation.1 | custom fusion | bytes 2176000 | tf_op jit(solution)/shard_map/gather | solution.py:23
  101.8 9.6 copy.116
  111.4 1.8 convolution_bitcast_fusion.3
  114.2 8.7 copy.118
  122.9 176.8 %scatter_custom_fusion = f32[8,20480]{0,1:T(8,128)} fusion(s32[32000]{0:T(1024)S(1)} %reshape.126, f32[32000,8]{1,0:T(8,128)} %copy.118, f32[]{:T(128)} %constant.9.clone.1), kind=kCustom, calls=%fused_computation.22 | custom fusion | flops 256000 | bytes 655872 | tf_op jit(solution)/shard_map/scatter-add | solution.py:27
  299.7 1.7 slice.99
  301.7 3.7 collective-permute-start.1
  309.4 5.7 slice.98
  315.2 2.0 copy.120
  317.2 27.0 %scatter_fusion = f32[8,16384]{0,1:T(8,128)} fusion(f32[8,16384]{0,1:T(8,128)} %slice.98, s32[4096]{0:T(1024)S(1)} %get-tuple-element.12, f32[4096,8]{1,0:T(8,128)} %copy.120), kind=kCustom, calls=%fused_computation.9 | custom fusion | flops 32768 | bytes 409600 | tf_op jit(solution)/shard_map/scatter-add | solution.py:30
  344.2 5.5 copy.121
  349.8 3.6 copy.122
  353.4 13.8 gather_fusion.2
  368.8 4.9 collective-permute-done.2
  373.7 5.4 copy.124
  379.1 63.1 %gather_fusion.3 = f32[32000,8]{1,0:T(8,128)} fusion(f32[8,20480]{0,1:T(8,128)} %copy.124, s32[32768]{0:T(1024)S(1)} %pad_clamp_fusion), kind=kCustom, calls=%fused_computation.3 | custom fusion | bytes 2176000 | tf_op jit(solution)/shard_map/gather | solution.py:23
  442.2 9.6 copy.125
  451.8 1.8 convolution_bitcast_fusion.2
  455.4 9.0 copy.127
  464.5 176.8 %scatter_custom_fusion.2 = f32[8,20480]{0,1:T(8,128)} fusion(s32[32000]{0:T(1024)S(1)} %reshape.126, f32[32000,8]{1,0:T(8,128)} %copy.127, f32[]{:T(128)} %constant.9.clone.1), kind=kCustom, calls=%fused_computation.20 | custom fusion | flops 256000 | bytes 655872 | tf_op jit(solution)/shard_map/scatter-add | solution.py:27
  641.3 1.7 slice.103
  643.3 4.7 collective-permute-start.3
  648.1 5.7 slice.102
  653.9 2.0 copy.129
  655.9 37.7 %scatter_fusion.1 = f32[8,16384]{0,1:T(8,128)} fusion(f32[8,16384]{0,1:T(8,128)} %slice.102, s32[4096]{0:T(1024)S(1)} %get-tuple-element.12, f32[4096,8]{1,0:T(8,128)} %copy.129), kind=kCustom, calls=%fused_computation.11 | custom fusion | flops 32768 | bytes 409600 | tf_op jit(solution)/shard_map/scatter-add | solution.py:30
  693.6 5.6 copy.130
  699.3 3.6 copy.131
  702.9 13.8 gather_fusion.4
  718.2 4.9 collective-permute-done.4
  723.2 5.4 copy.133
  728.6 63.1 %gather_fusion.5 = f32[32000,8]{1,0:T(8,128)} fusion(f32[8,20480]{0,1:T(8,128)} %copy.133, s32[32768]{0:T(1024)S(1)} %pad_clamp_fusion), kind=kCustom, calls=%fused_computation.5 | custom fusion | bytes 2176000 | tf_op jit(solution)/shard_map/gather | solution.py:23
  791.7 9.6 copy.134
  801.3 1.8 convolution_bitcast_fusion.1
  804.0 8.7 copy.136
  812.8 176.8 %scatter_custom_fusion.4 = f32[8,20480]{0,1:T(8,128)} fusion(s32[32000]{0:T(1024)S(1)} %reshape.126, f32[32000,8]{1,0:T(8,128)} %copy.136, f32[]{:T(128)} %constant.9.clone.1), kind=kCustom, calls=%fused_computation.18 | custom fusion | flops 256000 | bytes 655872 | tf_op jit(solution)/shard_map/scatter-add | solution.py:27
  989.6 1.7 slice.107
  991.6 4.1 collective-permute-start.5
  995.8 5.7 slice.106
  1001.5 2.0 copy.138
  1003.5 27.0 %scatter_fusion.2 = f32[8,16384]{0,1:T(8,128)} fusion(f32[8,16384]{0,1:T(8,128)} %slice.106, s32[4096]{0:T(1024)S(1)} %get-tuple-element.12, f32[4096,8]{1,0:T(8,128)} %copy.138), kind=kCustom, calls=%fused_computation.13 | custom fusion | flops 32768 | bytes 409600 | tf_op jit(solution)/shard_map/scatter-add | solution.py:30
  1030.5 5.5 copy.139
  1036.2 3.6 copy.140
  1039.8 13.8 gather_fusion.6
  1053.8 1.5 collective-permute-start.6
  1055.3 4.6 collective-permute-done.6
  1060.1 5.4 copy.142
  1065.4 63.1 %gather_fusion.7 = f32[32000,8]{1,0:T(8,128)} fusion(f32[8,20480]{0,1:T(8,128)} %copy.142, s32[32768]{0:T(1024)S(1)} %pad_clamp_fusion), kind=kCustom, calls=%fused_computation.7 | custom fusion | bytes 2176000 | tf_op jit(solution)/shard_map/gather | solution.py:23
  1128.5 9.6 copy.143
  1138.2 1.8 convolution_bitcast_fusion
  1141.8 9.0 copy.145
  1150.8 176.8 %scatter_custom_fusion.6 = f32[8,20480]{0,1:T(8,128)} fusion(s32[32000]{0:T(1024)S(1)} %reshape.126, f32[32000,8]{1,0:T(8,128)} %copy.145, f32[]{:T(128)} %constant.9.clone.1), kind=kCustom, calls=%fused_computation.16 | custom fusion | flops 256000 | bytes 655872 | tf_op jit(solution)/shard_map/scatter-add | solution.py:27
  1327.6 1.7 slice.111
  1329.6 4.0 collective-permute-start.7
  1333.8 5.7 slice.110
  1339.5 2.0 copy.147
  1341.5 27.0 %scatter_fusion.3 = f32[8,16384]{0,1:T(8,128)} fusion(f32[8,16384]{0,1:T(8,128)} %slice.110, s32[4096]{0:T(1024)S(1)} %get-tuple-element.12, f32[4096,8]{1,0:T(8,128)} %copy.147), kind=kCustom, calls=%fused_computation.15 | custom fusion | flops 32768 | bytes 409600 | tf_op jit(solution)/shard_map/scatter-add | solution.py:30
  1368.5 5.5 copy.148
  1375.1 33.3 %all-gather.3.cloned.1.call-done = bf16[64,16384]{1,0:T(8,128)(2,1)} async-done(((bf16[8,16384]{1,0:T(8,128)(2,1)}), bf16[64,16384]{1,0:T(8,128)(2,1)}) %all-gather.3.cloned.1.call-update) | async-done | bytes 2097168 | tf_op jit(solution)/shard_map/all_gather | solution.py:61
  1408.3 2.3 fusion.27
  1410.7 44.1 %all-gather = f32[256,64]{1,0:T(8,128)S(1)} all-gather(f32[8,64]{1,0:T(8,128)S(1)} %fusion.27), channel_id=2, replica_groups=mesh['space'=32,'state'=8] {'space'}, dimensions={0}, use_global_device_ids=true | all-gather | bytes 67584 | tf_op jit(solution)/shard_map/all_gather | solution.py:65
  (55 shorter events, 18.1 us)
Async XLA Ops:
  7.2 104.3 %copy-start = (f32[250,125]{1,0:T(8,128)S(1)}, f32[250,125]{1,0:T(8,128)}, u32[]{:S(2)}) copy-start(f32[250,125]{1,0:T(8,128)} %param.10) | copy-start | bytes 375004
  7.2 1401.2 %all-gather.3.cloned.1.call-start = ((), (), s32[]{:S(2)}) async-start(), calls=%async_computation | async-start | bytes 2359296 | tf_op jit(solution)/shard_map/all_gather | solution.py:61
  26.1 6.2 collective-permute-start
  122.9 182.5 %copy-start.2 = (f32[3]{0:T(128)S(1)}, f32[3]{0:T(128)}, u32[]{:S(2)}) copy-start(f32[3]{0:T(128)} %param.9) | copy-start | bytes 40
  301.7 13.4 collective-permute-start.1
  315.1 34.6 %copy-start.1 = (f32[8,16384]{1,0:T(8,128)S(1)}, f32[8,16384]{1,0:T(8,128)}, u32[]{:S(2)}) copy-start(f32[8,16384]{1,0:T(8,128)} %param.8) | copy-start | bytes 1572868
  367.5 6.2 collective-permute-start.2
  643.3 10.6 collective-permute-start.3
  716.9 6.2 collective-permute-start.4
  991.6 9.9 collective-permute-start.5
  1053.8 6.2 collective-permute-start.6
  1329.6 9.8 collective-permute-start.7
Sparse Core Ops, SparseCore 0:
  1375.2 33.0 all-gather.2
